TPU v7x, 256 devices: a whole 4x4x8 slice. The times are simulated.
256 devices in a mesh: dp: 32 (over y, z_lo, core), pos: 8 (over z_hi, x).
Axes of the slice: x: 4, y: 4, z: 8 (z_hi: 2, z_lo: 4; z = z_hi * 4 + z_lo), core: 2. Of those that a mesh axis runs over, the one named last changes fastest.
Arguments:
- inputs: bfloat16 [64, 2048, 512], P('dp', 'pos'), may hold values from -6 to 6
- pre_act: bfloat16 [64, 2048, 512], P('dp', 'pos'), may hold values from -6 to 6
- grad_out: bfloat16 [64, 2048, 512], P('dp', 'pos'), may hold values from -6 to 6
- weight: bfloat16 [512, 9, 512], P(('dp', 'pos')), may hold values from -0.09375 to 0.09375
Outputs:
- grad_input: bfloat16 [64, 2048, 512], P('dp', 'pos')
- grad_weight: float32 [512, 9, 512], P(('dp', 'pos'))
All inputs are finite; a program needn't handle non-finite values.
Results may differ from a plain program's by a relative error of at most 0.005.
Values may be sent and summed in bfloat16 or wider, within the bound.
A program may use at most 128 MiB of HBM per device.

v0:
```python
import jax
import jax.numpy as jnp
from jax import lax
from jax.sharding import PartitionSpec as P

K = 9


def padded_2(block, sides, width):
    for axis, dim in sides:
        count = lax.axis_size(axis)
        forward = [(i, i + 1) for i in range(count - 1)]
        backward = [(target, source) for source, target in forward]
        low = lax.ppermute(
            lax.slice_in_dim(block, block.shape[dim] - width, None, axis=dim), axis, forward
        )
        high = lax.ppermute(lax.slice_in_dim(block, 0, width, axis=dim), axis, backward)
        block = jnp.concatenate([low, block, high], axis=dim)
    return block


def partner(block, axis, distance):
    count = lax.axis_size(axis)
    route = []
    for low in range(count):
        high = low | 1 << distance
        if high != low and high < count:
            route += [(low, high), (high, low)]
    return lax.ppermute(block, axis, route)


def gelu_slope(values):
    cdf = 0.5 * (1.0 + lax.erf(values * 0.7071067811865476))
    return cdf + values * jnp.exp(-0.5 * values * values) * 0.3989422804014327


def on_device(inputs, pre_act, grad_out, weight):
    seq_count, length, chan_width = inputs.shape
    half_width = (K - 1) // 2
    grad_pre = (grad_out.astype(jnp.float32) * gelu_slope(pre_act.astype(jnp.float32))).astype(
        jnp.bfloat16
    )
    stacked = jnp.stack([inputs, grad_pre])
    padded = padded_2(stacked, (("pos", 2),), half_width)
    whole = lax.all_gather(weight, ("dp", "pos"), axis=0, tiled=True)
    bit_count = lax.axis_size("pos").bit_length() - 1
    mirrored = padded
    for bit_num in range(bit_count):
        mirrored = partner(mirrored, "pos", bit_num)
    reverse = jnp.flip(mirrored, axis=(2, 3))
    both_inputs = jnp.stack([padded[0], reverse[0]])
    both_grads = jnp.stack([padded[1], reverse[1]])
    total = jnp.zeros((2, seq_count, length, chan_width), jnp.float32)
    for offset in range(K):
        begin = K - 1 - offset
        total = total + jnp.einsum(
            "bsto,io->bsti",
            both_grads[:, :, begin : begin + length],
            whole[:, offset, :],
            preferred_element_type=jnp.float32,
        )
    returned = total[1]
    for bit_num in range(bit_count):
        returned = partner(returned, "pos", bit_num)
    grad_input = (total[0] + jnp.flip(returned, axis=(1, 2))).astype(jnp.bfloat16)
    centre_grads = both_grads[:, :, half_width : half_width + length]
    full_terms = jnp.stack(
        [
            jnp.einsum(
                "bsti,bsto->io",
                both_inputs[:, :, offset : offset + length],
                centre_grads,
                preferred_element_type=jnp.float32,
            )
            for offset in range(K)
        ],
        axis=1,
    )
    grad_weight = lax.psum_scatter(full_terms, ("dp", "pos"), scatter_dimension=0, tiled=True)
    return (grad_input, grad_weight)


def solution(mesh):
    placed = (
        P("dp", "pos", None),
        P("dp", "pos", None),
        P("dp", "pos", None),
        P(("dp", "pos"), None, None),
    )
    return jax.shard_map(
        on_device,
        mesh=mesh,
        in_specs=placed,
        out_specs=(P("dp", "pos", None), P(("dp", "pos"), None, None)),
        check_vma=False,
    )
```

profile of v0, /device:TPU:32, one launch (start us, length us, event | category | flops | bytes accessed | tf_op | source)
XLA Modules:
  0.0 1130.8 jit_solution(16518667106808815034)
XLA Ops:
  7.2 0.0 copy-start
  7.2 0.0 all-gather.2.cloned.1.call-start
  7.2 1.4 copy.15
  8.6 0.0 all-gather.2.cloned.1.call-update
  8.6 0.0 all-reduce.3.cloned.1.call-start
  8.7 1.7 fusion.60
  10.4 0.8 pad_maximum_fusion.6
  11.1 3.4 collective-permute-start
  14.5 1.3 collective-permute-start.1
  15.8 0.1 collective-permute-done
  16.0 4.2 collective-permute-done.1
  20.2 0.0 copy-done
  20.2 0.3 pad_maximum_fusion
  20.5 1.6 collective-permute-start.2
  22.1 22.7 %collective-permute-done.2 = bf16[2,2,264,512]{3,2,1,0:T(8,128)(2,1)S(1)} collective-permute-done((bf16[2,2,264,512]{3,2,1,0:T(8,128)(2,1)S(1)}, bf16[2,2,264,512]{3,2,1,0:T(8,128)(2,1)S(1)}, u32[]{:S(2)}, u32[]{:S(2)}) %collective-permute-start.2) | collective-permute-done | bytes 1081376 | tf_op jit(solution)/shard_map/ppermute | solution.py:29
  44.7 15.1 %collective-permute-start.3 = (bf16[2,2,264,512]{3,2,1,0:T(8,128)(2,1)S(1)}, bf16[2,2,264,512]{3,2,1,0:T(8,128)(2,1)S(1)}, u32[]{:S(2)}, u32[]{:S(2)}) collective-permute-start(bf16[2,2,264,512]{3,2,1,0:T(8,128)(2,1)S(1)} %collective-permute-done.2), channel_id=1, source_target_pairs={{0,2},{2,0},{1,3},{3,1},{4,6},{6,4},{5,7},{7,5},{8,10},{10,8},{9,1... | collective-permute-start | bytes 3244040 | tf_op jit(solution)/shard_map/ppermute | solution.py:29
  59.8 23.4 %collective-permute-done.3 = bf16[2,2,264,512]{3,2,1,0:T(8,128)(2,1)S(1)} collective-permute-done((bf16[2,2,264,512]{3,2,1,0:T(8,128)(2,1)S(1)}, bf16[2,2,264,512]{3,2,1,0:T(8,128)(2,1)S(1)}, u32[]{:S(2)}, u32[]{:S(2)}) %collective-permute-start.3) | collective-permute-done | bytes 1081376 | tf_op jit(solution)/shard_map/ppermute | solution.py:29
  83.2 0.0 collective-permute-start.4
  83.2 0.1 fusion.80
  83.3 52.7 %collective-permute-done.4 = bf16[2,2,264,512]{3,2,1,0:T(8,128)(2,1)S(1)} collective-permute-done((bf16[2,2,264,512]{3,2,1,0:T(8,128)(2,1)S(1)}, bf16[2,2,264,512]{3,2,1,0:T(8,128)(2,1)S(1)}, u32[]{:S(2)}, u32[]{:S(2)}) %collective-permute-start.4) | collective-permute-done | bytes 1081376 | tf_op jit(solution)/shard_map/ppermute | solution.py:29
  136.0 0.1 fusion.79
  136.1 3.1 slice.116
  139.3 3.1 slice.139
  142.4 0.3 fusion.47
  142.8 1.7 fusion.8
  144.5 1.7 fusion.7
  146.2 1.8 fusion.6
  148.0 1.8 fusion.5
  149.8 1.7 fusion.4
  151.5 1.7 fusion.3
  153.3 1.8 fusion.2
  155.1 1.7 fusion.1
  156.8 1.7 fusion
  158.5 0.0 all-reduce.3.cloned.1.call-update
  158.5 598.6 %all-gather.2.cloned.1.call-done = bf16[512,9,512]{2,1,0:T(8,128)(2,1)} async-done(((bf16[2,9,512]{2,1,0:T(8,128)(2,1)}), bf16[512,9,512]{2,1,0:T(8,128)(2,1)}) %all-gather.2.cloned.1.call-update) | async-done | bytes 4718608 | tf_op jit(solution)/shard_map/all_gather | solution.py:45
  757.2 19.3 %fusion.78 = (bf16[512,1,512]{2,1,0:T(2,128)(2,1)S(1)}, bf16[512,1,512]{2,1,0:T(2,128)(2,1)S(1)}, bf16[512,1,512]{2,1,0:T(2,128)(2,1)S(1)}, bf16[512,1,512]{2,1,...) fusion(bf16[512,9,512]{2,1,0:T(8,128)(2,1)} %all-gather.2.clone, ...), kind=kLoop, calls=%fused_computation.126 | loop fusion | bytes 9437184 | tf_op jit(solution)/shard_map/slice | solution.py:59
  776.5 0.7 fusion.36
  777.3 0.7 fusion.39
  778.0 0.8 fusion.42
  778.8 0.8 fusion.45
  779.5 0.7 fusion.49
  780.3 0.8 fusion.52
  781.1 0.8 fusion.33
  781.8 0.7 fusion.59
  782.6 1.6 add_add_fusion
  784.2 0.1 slice_bitcast_fusion
  784.2 0.1 collective-permute-start.5
  784.3 26.7 %collective-permute-done.5 = f32[2,256,512]{2,1,0:T(8,128)S(1)} collective-permute-done((f32[2,256,512]{2,1,0:T(8,128)S(1)}, f32[2,256,512]{2,1,0:T(8,128)S(1)}, u32[]{:S(2)}, u32[]{:S(2)}) %collective-permute-start.5) | collective-permute-done | bytes 1048608 | tf_op jit(solution)/shard_map/ppermute | solution.py:29
  811.0 0.0 collective-permute-start.6
  811.0 31.8 %collective-permute-done.6 = f32[2,256,512]{2,1,0:T(8,128)S(1)} collective-permute-done((f32[2,256,512]{2,1,0:T(8,128)S(1)}, f32[2,256,512]{2,1,0:T(8,128)S(1)}, u32[]{:S(2)}, u32[]{:S(2)}) %collective-permute-start.6) | collective-permute-done | bytes 1048608 | tf_op jit(solution)/shard_map/ppermute | solution.py:29
  842.8 4.8 collective-permute-start.7
  847.5 266.4 %all-reduce.3.cloned.1.call-done = f32[512,9,512]{2,0,1:T(8,128)} async-done(((f32[512,9,512]{2,0,1:T(8,128)}), f32[512,9,512]{2,0,1:T(8,128)}) %all-reduce.3.cloned.1.call-update) | async-done | bytes 9437200
  1113.9 1.5 constant_dynamic-slice_fusion
  1115.5 0.0 collective-permute-done.7
  1115.5 7.5 rev.6
  1123.0 1.0 fusion.56
Async XLA Ops:
  7.2 13.0 %copy-start = (bf16[2,256,512]{2,1,0:T(8,128)(2,1)S(1)}, bf16[2,256,512]{2,1,0:T(8,128)(2,1)}, u32[]{:S(2)}) copy-start(bf16[2,256,512]{2,1,0:T(8,128)(2,1)} %param.4) | copy-start | bytes 1572868
  7.2 750.0 %all-gather.2.cloned.1.call-start = ((), (), s32[]{:S(2)}) async-start(), calls=%async_computation | async-start | bytes 8421376 | tf_op jit(solution)/shard_map/all_gather | solution.py:45
  8.6 1105.3 %all-reduce.3.cloned.1.call-start = ((), (), s32[]{:S(2)}) async-start(), calls=%async_computation.1 | async-start | bytes 18874368
  11.1 4.8 collective-permute-start
  14.5 5.6 collective-permute-start.1
  20.5 24.3 %collective-permute-start.2 = (bf16[2,2,264,512]{3,2,1,0:T(8,128)(2,1)S(1)}, bf16[2,2,264,512]{3,2,1,0:T(8,128)(2,1)S(1)}, u32[]{:S(2)}, u32[]{:S(2)}) collective-permute-start(bf16[2,2,264,512]{3,2,1,0:T(8,128)(2,1)S(1)} %pad_maximum_fusion), channel_id=1, source_target_pairs={{0,1},{1,0},{2,3},{3,2},{4,5},{5,4},{6,7},{7,6},{8,9},{9,8},{10,11... | collective-permute-start | bytes 3244040 | tf_op jit(solution)/shard_map/ppermute | solution.py:29
  44.7 38.5 %collective-permute-start.3 = (bf16[2,2,264,512]{3,2,1,0:T(8,128)(2,1)S(1)}, bf16[2,2,264,512]{3,2,1,0:T(8,128)(2,1)S(1)}, u32[]{:S(2)}, u32[]{:S(2)}) collective-permute-start(bf16[2,2,264,512]{3,2,1,0:T(8,128)(2,1)S(1)} %collective-permute-done.2), channel_id=1, source_target_pairs={{0,2},{2,0},{1,3},{3,1},{4,6},{6,4},{5,7},{7,5},{8,10},{10,8},{9,1... | collective-permute-start | bytes 3244040 | tf_op jit(solution)/shard_map/ppermute | solution.py:29
  83.2 52.8 %collective-permute-start.4 = (bf16[2,2,264,512]{3,2,1,0:T(8,128)(2,1)S(1)}, bf16[2,2,264,512]{3,2,1,0:T(8,128)(2,1)S(1)}, u32[]{:S(2)}, u32[]{:S(2)}) collective-permute-start(bf16[2,2,264,512]{3,2,1,0:T(8,128)(2,1)S(1)} %collective-permute-done.3), channel_id=1, source_target_pairs={{0,4},{4,0},{1,5},{5,1},{2,6},{6,2},{3,7},{7,3},{8,12},{12,8},{9,1... | collective-permute-start | bytes 3244040 | tf_op jit(solution)/shard_map/ppermute | solution.py:29
  784.2 26.8 %collective-permute-start.5 = (f32[2,256,512]{2,1,0:T(8,128)S(1)}, f32[2,256,512]{2,1,0:T(8,128)S(1)}, u32[]{:S(2)}, u32[]{:S(2)}) collective-permute-start(f32[2,256,512]{2,1,0:T(8,128)S(1)} %slice_bitcast_fusion), channel_id=1, source_target_pairs={{0,1},{1,0},{2,3},{3,2},{4,5},{5,4},{6,7},{7,6},{8,9},{9,8},{10,11... | collective-permute-start | bytes 3145736 | tf_op jit(solution)/shard_map/ppermute | solution.py:29
  811.0 31.8 %collective-permute-start.6 = (f32[2,256,512]{2,1,0:T(8,128)S(1)}, f32[2,256,512]{2,1,0:T(8,128)S(1)}, u32[]{:S(2)}, u32[]{:S(2)}) collective-permute-start(f32[2,256,512]{2,1,0:T(8,128)S(1)} %collective-permute-done.5), channel_id=1, source_target_pairs={{0,2},{2,0},{1,3},{3,1},{4,6},{6,4},{5,7},{7,5},{8,10},{10,8},{9,1... | collective-permute-start | bytes 3145736 | tf_op jit(solution)/shard_map/ppermute | solution.py:29
  842.8 272.7 %collective-permute-start.7 = (f32[2,256,512]{2,1,0:T(8,128)S(1)}, f32[2,256,512]{2,1,0:T(8,128)}, u32[]{:S(2)}, u32[]{:S(2)}) collective-permute-start(f32[2,256,512]{2,1,0:T(8,128)S(1)} %collective-permute-done.6), channel_id=1, source_target_pairs={{0,4},{4,0},{1,5},{5,1},{2,6},{6,2},{3,7},{7,3},{8,12},{12,8},{9,1... | collective-permute-start | bytes 3145736 | tf_op jit(solution)/shard_map/ppermute | solution.py:29
Sparse Core Ops, SparseCore 0:
  10.5 746.6 all-gather.1
  762.8 351.1 all-reduce.2
where the time goes:
time: 1130 us
  waiting for transfers between devices  1030 us (91%)
  local copies, waits for them, and re-layouts  36.3 us (3%)
  starting transfers between devices  26.3 us (2%)
  matrix products  23.3 us (2%)
  between operations  14.2 us (1%)
    all_gather x1, waiting for transfers between devices, on_device(): whole = lax.all_gather(weight, ('dp', 'pos'), axis=0, tiled=True)  599 us
    unnamed x3, waiting for transfers between devices  266 us
    ppermute x6, waiting for transfers between devices, partner(): return lax.ppermute(block, axis, route)  157 us
  transfers between devices with their start and end apart: 10, of which 9 were waited for; matrix products, arithmetic and copies ran while one was open for 5% of the time, Pallas kernels for 0%

commit v1 on v0

v1 whole, which is shorter than its diff:
```python
import jax
import jax.numpy as jnp
import numpy as np
from jax import lax
from jax.experimental import pallas as pl
from jax.experimental.pallas import tpu as pltpu
from jax.sharding import PartitionSpec as P

K = 9
HALO = 8
GROUPS = 3
TAPS = K // GROUPS
MESH = pl.DeviceIdType.MESH
F32 = jnp.float32
BF16 = jnp.bfloat16


def gelu_slope(values):
    cdf = 0.5 * (1.0 + lax.erf(values * 0.7071067811865476))
    return cdf + values * jnp.exp(-0.5 * values * values) * 0.3989422804014327


def device(x, y, z, c):
    return ((y * 4 + z % 4) * 2 + c, (z // 4) * 4 + x)


def channel_orders():
    sorts = np.zeros((2, 512, 512), np.float32)
    for core in range(2):
        for q in range(4):
            for p in range(4):
                x, y = (p, q) if core == 0 else (q, p)
                for z in range(8):
                    for c in range(2):
                        row = (q * 4 + p) * 16 + 2 * z + c
                        dp, pos = device(x, y, z, c)
                        even = 2 * (dp * 8 + pos)
                        sorts[core, row, even] = 1.0
                        sorts[core, 256 + row, 511 - even] = 1.0
    return sorts.astype(jnp.bfloat16)


def dot(a, b, ca, cb):
    return lax.dot_general(a, b, (((ca,), (cb,)), ((), ())), preferred_element_type=F32)


def kernel(
    w_ref, pre_hbm, go_hbm, x_hbm, sort_hbm, gi_hbm, gw_hbm,
    pv, gv, xv, sv, gp, gfp, xt, rk, edge_out, edge_in,
    mirror_out, mirror_in, zb, wb_own, wb_oth,
    sf, sd, dr, qs, qr, t1, ps, pr, zs, zr, fs, fr, ow, acc, eo, gi,
    load_sem, store_sem, m_s, m_r, h_s, h_r, z_s, z_r, p_s, p_r, q_s, q_r, d_s, d_r,
    rd_s, rd_r, rq_s, rq_r, rp_s, rp_r, rz_s, rz_r, f_s, f_r,
):
    dp, pos = lax.axis_index("dp"), lax.axis_index("pos")
    y, c = dp // 8, dp % 2
    x = pos % 4
    z = (pos // 4) * 4 + (dp // 2) % 4
    p = x * (1 - c) + y * c
    q = y * (1 - c) + x * c
    z_peers = [device(x, y, (z + i) % 8, c) for i in range(1, 8)]
    p_peers = [device((x + i * (1 - c)) % 4, (y + i * c) % 4, z, c) for i in range(1, 4)]
    q_peers = [device((x + i * c) % 4, (y + i * (1 - c)) % 4, z, c) for i in range(1, 4)]
    twin = device(x, y, z, 1 - c)
    mirror_a = device(3 - x, 3 - y, 7 - z, 1 - c)
    mirror_b = device(3 - x, 3 - y, 7 - z, c)
    after, before = (dp, (pos + 1) % 8), (dp, (pos + 7) % 8)

    barrier = pltpu.get_barrier_semaphore()
    peers = z_peers + p_peers + q_peers + [twin, mirror_a, mirror_b, after, before]
    for peer in peers:
        pl.semaphore_signal(barrier, inc=1, device_id=peer, device_id_type=MESH)

    own_lanes = pl.ds(pl.multiple_of(c * 256, 256), 256)
    oth_lanes = pl.ds(pl.multiple_of((1 - c) * 256, 256), 256)
    loads = [
        pltpu.make_async_copy(pre_hbm.at[:, :, own_lanes], pv.at[0], load_sem.at[0]),
        pltpu.make_async_copy(go_hbm.at[:, :, own_lanes], gv.at[0], load_sem.at[1]),
        pltpu.make_async_copy(pre_hbm.at[:, :, oth_lanes], pv.at[1], load_sem.at[2]),
        pltpu.make_async_copy(go_hbm.at[:, :, oth_lanes], gv.at[1], load_sem.at[3]),
        pltpu.make_async_copy(x_hbm, xv, load_sem.at[4]),
        pltpu.make_async_copy(sort_hbm.at[c], sv, load_sem.at[5]),
    ]
    for load in loads:
        load.start()

    sends = []

    def send(src, dst, send_sem, recv_sem, peer):
        copy = pltpu.make_async_remote_copy(
            src_ref=src, dst_ref=dst, send_sem=send_sem, recv_sem=recv_sem,
            device_id=peer, device_id_type=MESH,
        )
        copy.start()
        sends.append(copy)
        return copy

    rows_i = lax.broadcasted_iota(jnp.int32, (256, 256), 0)
    cols_i = lax.broadcasted_iota(jnp.int32, (256, 256), 1)
    flip = jnp.where(rows_i + cols_i == 255, 1.0, 0.0).astype(BF16)

    w0_own = w_ref[0, :, own_lanes].astype(F32)
    mirror_out[0] = w_ref[1, :, own_lanes].astype(F32)
    mirror_out[1] = w_ref[1, :, oth_lanes].astype(F32)
    mirror_out[2] = w_ref[0, :, oth_lanes].astype(F32)

    zeros = jnp.zeros((2, HALO, 512), F32)
    for padded in (gp, gfp):
        padded[:, 0:HALO, :] = zeros
        padded[:, HALO + 256 : 2 * HALO + 256, :] = zeros
    for half in range(2):
        loads[2 * half].wait()
        loads[2 * half + 1].wait()
        for seq in range(2):

            def slope(i, carry, half=half, seq=seq):
                rows = pl.ds(pl.multiple_of(i * 32, 32), 32)
                values = pv[half, seq, rows, :].astype(F32)
                grad = gv[half, seq, rows, :].astype(F32) * gelu_slope(values)
                place = pl.ds(pl.multiple_of(HALO + i * 32, 8), 32)
                gp[seq, place, half * 256 : half * 256 + 256] = grad.astype(BF16).astype(F32)
                return carry

            lax.fori_loop(0, 8, slope, 0)
    edge_out[0] = gp[:, 256 : 256 + HALO, :]
    edge_out[1] = gp[:, HALO : 2 * HALO, :]

    pl.semaphore_wait(barrier, len(peers))
    mirror = [
        send(mirror_out.at[i], mirror_in.at[i], m_s.at[i], m_r.at[i], peer)
        for i, peer in enumerate((mirror_a, mirror_b, twin))
    ]
    edges = [
        send(edge_out.at[i], edge_in.at[i], h_s.at[i], h_r.at[i], peer)
        for i, peer in enumerate((after, before))
    ]

    for seq in range(2):
        main = gp[seq, HALO : HALO + 256, :].astype(BF16)
        gfp[seq, HALO : HALO + 256, 0:256] = dot(main[:, 256:512], flip, 1, 0)
        gfp[seq, HALO : HALO + 256, 256:512] = dot(main[:, 0:256], flip, 1, 0)
    loads[4].wait()
    loads[5].wait()
    for seq in range(2):
        sorted_x = dot(sv[...], xv[seq], 1, 1).astype(BF16)
        xt[:, seq * 256 : seq * 256 + 256] = sorted_x[0:256]
        xt[:, 512 + seq * 256 : 768 + seq * 256] = sorted_x[256:512]
    for k in range(K):
        for seq in range(2):
            rk[k, seq * 256 : seq * 256 + 256, :] = gp[seq, 12 - k : 268 - k, :].astype(BF16)
            rk[k, 512 + seq * 256 : 768 + seq * 256, :] = gfp[seq, 4 + k : 260 + k, :].astype(BF16)

    for copy in mirror:
        copy.wait_recv()
    rev_a = dot(mirror_in[0].astype(BF16), flip, 1, 0)
    rev_b = dot(mirror_in[1].astype(BF16), flip, 1, 0)
    w0_oth = mirror_in[2]
    for k in range(K):
        zb[k, pl.ds(2 * z + c, 1), :] = w0_own[k : k + 1] + rev_a[8 - k : 9 - k]
        zb[k, pl.ds(2 * z + 1 - c, 1), :] = w0_oth[k : k + 1] + rev_b[8 - k : 9 - k]
    mine = pl.ds(2 * z, 2)
    z_gather = [
        send(zb.at[:, mine, :], zb.at[:, mine, :], z_s.at[i], z_r.at[i], peer)
        for i, peer in enumerate(z_peers)
    ]

    for copy in edges:
        copy.wait_recv()
    low = jnp.where(pos == 0, 0.0, edge_in[0])
    high = jnp.where(pos == 7, 0.0, edge_in[1])
    gp[:, 0:HALO, :] = low
    gp[:, HALO + 256 : 2 * HALO + 256, :] = high
    both = jnp.concatenate([low[0], low[1], high[0], high[1]], axis=0).astype(BF16)
    both = jnp.concatenate(
        [dot(both[:, 256:512], flip, 1, 0), dot(both[:, 0:256], flip, 1, 0)], axis=1
    )
    for seq in range(2):
        gfp[seq, 0:HALO, :] = both[seq * HALO : seq * HALO + HALO]
        gfp[seq, HALO + 256 : 2 * HALO + 256, :] = both[(2 + seq) * HALO : (3 + seq) * HALO]
    for k in range(K):
        for seq in range(2):
            for start in (0, 240):
                rk[k, seq * 256 + start : seq * 256 + start + 16, :] = gp[
                    seq, 12 - k + start : 28 - k + start, :
                ].astype(BF16)
                rk[k, 512 + seq * 256 + start : 528 + seq * 256 + start, :] = gfp[
                    seq, 4 + k + start : 20 + k + start, :
                ].astype(BF16)

    def products(group):
        def one(k, carry):
            terms = dot(xt[...], rk[k], 1, 0)
            for a in range(4):
                for b in range(4):
                    rows = slice((a * 4 + b) * 16, (a * 4 + b) * 16 + 16)
                    sf[k, a, b] = terms[rows, 0:256]
                    sd[k, b, a] = terms[rows, 256:512].astype(BF16)
            return carry

        lax.fori_loop(group * TAPS, group * TAPS + TAPS, one, 0)
        taps = pl.ds(group * TAPS, TAPS)
        return send(sd.at[taps], dr.at[taps], rd_s.at[group], rd_r.at[group], twin)

    def chip_sum(group, copy):
        copy.wait_recv()

        def one(k, carry):
            total = sf[k] + dr[k].astype(F32)
            sf[k] = total
            qs[k] = total.astype(BF16)
            return carry

        lax.fori_loop(group * TAPS, group * TAPS + TAPS, one, 0)
        taps = pl.ds(group * TAPS, TAPS)
        return [
            send(
                qs.at[taps, (q + i) % 4], qr.at[i - 1, taps],
                rq_s.at[group, i - 1], rq_r.at[group, i - 1], q_peers[i - 1],
            )
            for i in range(1, 4)
        ]

    def q_sum(group, copies):
        for copy in copies:
            copy.wait_recv()

        def one(k, carry):
            total = sf[k, q] + qr[0, k].astype(F32) + qr[1, k].astype(F32) + qr[2, k].astype(F32)
            t1[k] = total
            ps[k] = total.astype(BF16)
            return carry

        lax.fori_loop(group * TAPS, group * TAPS + TAPS, one, 0)
        taps = pl.ds(group * TAPS, TAPS)
        return [
            send(
                ps.at[taps, (p + i) % 4], pr.at[i - 1, taps],
                rp_s.at[group, i - 1], rp_r.at[group, i - 1], p_peers[i - 1],
            )
            for i in range(1, 4)
        ]

    q_copies = []
    twin_copy = products(0)
    for group in range(1, GROUPS):
        next_copy = products(group)
        q_copies.append(chip_sum(group - 1, twin_copy))
        twin_copy = next_copy
    q_copies.append(chip_sum(GROUPS - 1, twin_copy))

    for copy in z_gather:
        copy.wait_recv()
    wb_own[:, q, p] = zb[...].astype(BF16)
    p_gather = [
        send(wb_own.at[:, q, p], wb_own.at[:, q, p], p_s.at[i], p_r.at[i], peer)
        for i, peer in enumerate(p_peers)
    ]
    p_copies = [q_sum(0, q_copies[0])]
    for copy in p_gather:
        copy.wait_recv()
    q_gather = [
        send(wb_own.at[:, q], wb_own.at[:, q], q_s.at[i], q_r.at[i], peer)
        for i, peer in enumerate(q_peers)
    ]
    d_gather = [send(wb_own.at[:, q], wb_oth.at[:, q], d_s.at[0], d_r.at[0], twin)]
    for group in range(1, GROUPS):
        p_copies.append(q_sum(group, q_copies[group]))
    for group in range(GROUPS):
        for copy in p_copies[group]:
            copy.wait_recv()

    def p_sum(k, carry):
        zs[k] = t1[k, p] + pr[0, k].astype(F32) + pr[1, k].astype(F32) + pr[2, k].astype(F32)
        return carry

    lax.fori_loop(0, K, p_sum, 0)
    z_scatter = [
        send(
            zs.at[:, pl.ds(2 * ((z + i) % 8), 2), :], zr.at[i - 1, :, pl.ds(2 * ((z + i) % 8), 2), :],
            rz_s.at[i - 1], rz_r.at[i - 1], z_peers[i - 1],
        )
        for i in range(1, 8)
    ]

    for i in range(1, 4):
        q_gather[i - 1].wait_recv()
        from_q = (q + 4 - i) % 4
        d_gather.append(
            send(wb_own.at[:, from_q], wb_oth.at[:, from_q], d_s.at[i], d_r.at[i], twin)
        )

    def input_own(m, carry):
        rows = pl.ds(pl.multiple_of(m * 256, 256), 256)
        total = jnp.zeros((256, 256), F32)
        for k in range(K):
            total = total + dot(rk[k, rows, 0:256], wb_own[k].reshape(256, 256), 1, 1)
        acc[rows, :] = total
        return carry

    lax.fori_loop(0, 4, input_own, 0)

    for copy in z_scatter:
        copy.wait_recv()
    for row, place in enumerate((2 * z + c, 2 * z + 1 - c)):
        total = zs[:, pl.ds(place, 1), :]
        for i in range(7):
            total = total + zr[i, :, pl.ds(place, 1), :]
        for k in range(K):
            fs[row, k : k + 1, :] = total[k]
    final = [
        send(fs.at[1], fr.at[0], f_s.at[0], f_r.at[0], twin),
        send(fs.at[0], fr.at[1], f_s.at[1], f_r.at[1], mirror_a),
        send(fs.at[1], fr.at[2], f_s.at[2], f_r.at[2], mirror_b),
    ]

    for copy in d_gather:
        copy.wait_recv()

    def other_weight(k):
        return jnp.concatenate([wb_oth[k, b, a] for a in range(4) for b in range(4)], axis=0)

    def input_oth(m, carry):
        rows = pl.ds(pl.multiple_of(m * 256, 256), 256)
        total = acc[rows, :]
        for k in range(K):
            total = total + dot(rk[k, rows, 256:512], other_weight(k), 1, 1)
        acc[rows, :] = total
        return carry

    lax.fori_loop(0, 4, input_oth, 0)
    stores = []
    for seq in range(2):
        eo[:, 0:256] = acc[seq * 256 : seq * 256 + 256, :].astype(BF16)
        eo[:, 256:512] = acc[512 + seq * 256 : 768 + seq * 256, :].astype(BF16)
        gi[seq] = dot(eo[...], sv[...], 1, 0).astype(BF16)
        store = pltpu.make_async_copy(gi.at[seq], gi_hbm.at[seq], store_sem.at[seq])
        store.start()
        stores.append(store)

    for copy in final:
        copy.wait_recv()
    ow[0, 0] = fs[0]
    ow[1, 0] = fr[0]
    for half in range(2):
        value = fr[1 + half]
        high = value.astype(BF16)
        rest = value - high.astype(F32)
        mid = rest.astype(BF16)
        low = (rest - mid.astype(F32)).astype(BF16)
        reverse = dot(high, flip, 1, 0) + dot(mid, flip, 1, 0) + dot(low, flip, 1, 0)
        for k in range(K):
            ow[half, 1, k : k + 1, :] = reverse[8 - k : 9 - k]
    for half, lanes in enumerate((own_lanes, oth_lanes)):
        store = pltpu.make_async_copy(ow.at[half], gw_hbm.at[:, :, lanes], store_sem.at[2 + half])
        store.start()
        stores.append(store)
    for copy in sends:
        copy.wait_send()
    for store in stores:
        store.wait()


def on_device(inputs, pre_act, grad_out, weight):
    sorts = jnp.asarray(channel_orders())
    dma = pltpu.SemaphoreType.DMA
    vmem = pltpu.VMEM
    return pl.pallas_call(
        kernel,
        out_shape=(
            jax.ShapeDtypeStruct((2, 256, 512), BF16),
            jax.ShapeDtypeStruct((2, K, 512), F32),
        ),
        in_specs=[pl.BlockSpec(memory_space=vmem)] + [pl.BlockSpec(memory_space=pl.ANY)] * 4,
        out_specs=[pl.BlockSpec(memory_space=pl.ANY)] * 2,
        scratch_shapes=[
            vmem((2, 2, 256, 256), BF16),
            vmem((2, 2, 256, 256), BF16),
            vmem((2, 256, 512), BF16),
            vmem((512, 512), BF16),
            vmem((2, 256 + 2 * HALO, 512), F32),
            vmem((2, 256 + 2 * HALO, 512), F32),
            vmem((256, 1024), BF16),
            vmem((K, 1024, 512), BF16),
            vmem((2, 2, HALO, 512), F32),
            vmem((2, 2, HALO, 512), F32),
            vmem((3, K, 256), F32),
            vmem((3, K, 256), F32),
            vmem((K, 16, 256), F32),
            vmem((K, 4, 4, 16, 256), BF16),
            vmem((K, 4, 4, 16, 256), BF16),
            vmem((K, 4, 4, 16, 256), F32),
            vmem((K, 4, 4, 16, 256), BF16),
            vmem((K, 4, 4, 16, 256), BF16),
            vmem((K, 4, 4, 16, 256), BF16),
            vmem((3, K, 4, 16, 256), BF16),
            vmem((K, 4, 16, 256), F32),
            vmem((K, 4, 16, 256), BF16),
            vmem((3, K, 16, 256), BF16),
            vmem((K, 16, 256), F32),
            vmem((7, K, 16, 256), F32),
            vmem((2, K, 256), F32),
            vmem((3, K, 256), F32),
            vmem((2, 2, K, 256), F32),
            vmem((1024, 256), F32),
            vmem((256, 512), BF16),
            vmem((2, 256, 512), BF16),
            dma((6,)), dma((4,)),
            dma((3,)), dma((3,)), dma((2,)), dma((2,)), dma((7,)), dma((7,)),
            dma((3,)), dma((3,)), dma((3,)), dma((3,)), dma((4,)), dma((4,)),
            dma((GROUPS,)), dma((GROUPS,)), dma((GROUPS, 3)), dma((GROUPS, 3)),
            dma((GROUPS, 3)), dma((GROUPS, 3)), dma((7,)), dma((7,)), dma((3,)), dma((3,)),
        ],
        compiler_params=pltpu.CompilerParams(
            collective_id=0, has_side_effects=True, vmem_limit_bytes=56 << 20
        ),
        name="conv_backward",
    )(weight, pre_act, grad_out, inputs, sorts)


def solution(mesh):
    placed = (
        P("dp", "pos", None),
        P("dp", "pos", None),
        P("dp", "pos", None),
        P(("dp", "pos"), None, None),
    )
    return jax.shard_map(
        on_device,
        mesh=mesh,
        in_specs=placed,
        out_specs=(P("dp", "pos", None), P(("dp", "pos"), None, None)),
        check_vma=False,
    )
```

time: 1130 us -> 56.2 us (0.05)
  waiting for transfers between devices: 1030 us -> 0 us
  Pallas kernels: 0 us -> 50.5 us
  local copies, waits for them, and re-layouts: 36.3 us -> 4.7 us
  starting transfers between devices: 26.3 us -> 0 us
  matrix products: 23.3 us -> 0 us
  between operations: 14.2 us -> 0.64 us
    all_gather x1 -> x0, waiting for transfers between devices: 599 us -> none  [on_device(): whole = lax.all_gather(weight, ('dp', 'pos'), axis=0, tiled=True)]
    unnamed x3 -> x0, waiting for transfers between devices: 266 us -> none
    ppermute x8 -> x0, waiting for transfers between devices: 162 us -> none  [the longest x6 157 us: partner(): return lax.ppermute(block, axis, route)]
    pallas_call x0 -> x1, Pallas kernels: none -> 50.5 us  [on_device(): pl.pallas_call(kernel, out_shape=(jax.ShapeDtypeStruct((2, 256, 512), BF1...]
    ppermute x8 -> x0, starting transfers between devices: 26.2 us -> none  [the longest x6 21.5 us: partner(): return lax.ppermute(block, axis, route)]
    slice x5 -> x0, local copies, waits for them, and re-layouts: 25.8 us -> none  [the longest x1 19.3 us: on_device(): whole[:, offset, :]]
    dot_general x18 -> x0, matrix products: 23.3 us -> none  [the longest x9 15.7 us: on_device(): jnp.einsum('bsti,bsto->io', both_inputs[:, :, offset:offset + length], ce...]
  transfers between devices with their start and end apart: 10 -> 0, of which waited for: 9 -> 0; matrix products, arithmetic and copies ran while one was open for 5% -> 0% of each run, Pallas kernels for 0% -> 0%
where the time goes in v1:
time: 56.2 us; the launch traced here: 55.8 us
  Pallas kernels  50.5 us (90%)
  local copies, waits for them, and re-layouts  4.7 us (8%)
  between operations  0.64 us (1%)
    pallas_call x1, Pallas kernels, on_device(): pl.pallas_call(kernel, out_shape=(jax.ShapeDtypeStruct((2, 256, 512), BF1...  50.5 us
    unnamed x2, local copies, waits for them, and re-layouts  3.21 us
    pallas_call x1, local copies, waits for them, and re-layouts, on_device(): pl.pallas_call(kernel, out_shape=(jax.ShapeDtypeStruct((2, 256, 512), BF1...  1.49 us

profile of v1, /device:TPU:32, one launch (start us, length us, event | category | flops | bytes accessed | tf_op | source)
XLA Modules:
  0.0 55.8 jit_solution(14858381267795286260)
XLA Ops:
  0.6 1.3 %copy.7.w_ref = bf16[2,9,512]{2,1,0:T(8,128)(2,1)} copy(bf16[2,9,512]{2,0,1:T(2,128)(2,1)} %param.8) | data formatting | bytes 36864 | tf_op args[3]
  2.0 50.5 %conv_backward.1 = (bf16[2,256,512]{2,1,0:T(8,128)(2,1)}, f32[2,9,512]{2,1,0:T(8,128)}) custom-call(bf16[2,9,512]{2,1,0:T(8,128)(2,1)} %copy.7.w_ref, bf16[2,256,512]{2,1,0:T(8,128)(2,1)} %pre_hbm.1, bf16[2,256,512]{2,1,0:T(8,128)(2,1)} %go_hbm.1, bf16[2,256,512]{2,1,0:T(8,128)(2,1)} %x_hbm.1, bf16[2,512,512]{2,1,0:T(8,128)(2,1)} %constant.2.clone.sort_hbm), custom_call_target="tpu_custom_call" | custom-call | tf_op jit(solution)/shard_map/conv_backward/pallas_call | solution.py:367
  52.5 1.5 %copy.8 = f32[2,9,512]{2,0,1:T(2,128)} copy(f32[2,9,512]{2,1,0:T(8,128)} %get-tuple-element.3) | data formatting | bytes 73728 | tf_op jit(solution)/shard_map/conv_backward/pallas_call | solution.py:367
  53.9 1.9 %copy.10 = bf16[2,256,512]{2,1,0:T(8,128)(2,1)} copy(bf16[2,256,512]{2,1,0:T(8,128)(2,1)} %get-tuple-element.6) | data formatting | bytes 1048576

commit v2 on v1

v2 whole, which is shorter than its diff:
```python
import jax
import jax.numpy as jnp
import numpy as np
from jax import lax
from jax.experimental import pallas as pl
from jax.experimental.pallas import tpu as pltpu
from jax.sharding import PartitionSpec as P

K = 9
HALO = 8
GROUPS = 3
TAPS = K // GROUPS
MESH = pl.DeviceIdType.MESH
F32 = jnp.float32
BF16 = jnp.bfloat16


def gelu_slope(values):
    cdf = 0.5 * (1.0 + lax.erf(values * 0.7071067811865476))
    return cdf + values * jnp.exp(-0.5 * values * values) * 0.3989422804014327


def device(x, y, z, c):
    return ((y * 4 + z % 4) * 2 + c, (z // 4) * 4 + x)


def channel_orders():
    sorts = np.zeros((2, 512, 512), np.float32)
    for core in range(2):
        for q in range(4):
            for p in range(4):
                x, y = (p, q) if core == 0 else (q, p)
                for z in range(8):
                    for c in range(2):
                        row = (q * 4 + p) * 16 + 2 * z + c
                        dp, pos = device(x, y, z, c)
                        even = 2 * (dp * 8 + pos)
                        sorts[core, row, even] = 1.0
                        sorts[core, 256 + row, 511 - even] = 1.0
    return sorts.astype(jnp.bfloat16)


def dot(a, b, ca, cb):
    return lax.dot_general(a, b, (((ca,), (cb,)), ((), ())), preferred_element_type=F32)


def kernel(
    w_ref, pre_hbm, go_hbm, x_hbm, sort_hbm, gi_hbm, gw_hbm,
    pv, gv, xv, sv, gp, gfp, xt, xe, x_out, x_in, rk, edge_out, edge_in, edge_pad, edge_rows,
    mirror_out, mirror_in, zb, wb_own, wb_oth,
    sf, sd, dr, qs, qr, t1, ps, pr, zs, zr, fs, fr, ow, acc, eo, gi,
    load_sem, store_sem, m_s, m_r, h_s, h_r, x_s, x_r, z_s, z_r, p_s, p_r, q_s, q_r, d_s, d_r,
    rd_s, rd_r, rq_s, rq_r, rp_s, rp_r, rz_s, rz_r, f_s, f_r,
):
    dp, pos = lax.axis_index("dp"), lax.axis_index("pos")
    y, c = dp // 8, dp % 2
    x = pos % 4
    z = (pos // 4) * 4 + (dp // 2) % 4
    p = x * (1 - c) + y * c
    q = y * (1 - c) + x * c
    z_steps = (4, 3, 5, 2, 6, 1, 7)
    z_peers = [device(x, y, (z + i) % 8, c) for i in z_steps]
    p_peers = [device((x + i * (1 - c)) % 4, (y + i * c) % 4, z, c) for i in range(1, 4)]
    q_peers = [device((x + i * c) % 4, (y + i * (1 - c)) % 4, z, c) for i in range(1, 4)]
    twin = device(x, y, z, 1 - c)
    mirror_a = device(3 - x, 3 - y, 7 - z, 1 - c)
    mirror_b = device(3 - x, 3 - y, 7 - z, c)
    other = dp + 1 - 2 * c
    beside = [(row, place) for place in ((pos + 1) % 8, (pos + 7) % 8) for row in (dp, other)]

    barrier = pltpu.get_barrier_semaphore()
    peers = [mirror_a, mirror_b] + beside + z_peers + p_peers + q_peers + [twin]
    for peer in peers:
        pl.semaphore_signal(barrier, inc=1, device_id=peer, device_id_type=MESH)

    own_lanes = pl.ds(pl.multiple_of(c * 256, 256), 256)
    oth_lanes = pl.ds(pl.multiple_of((1 - c) * 256, 256), 256)
    loads = [
        pltpu.make_async_copy(pre_hbm.at[:, :, own_lanes], pv.at[0], load_sem.at[0]),
        pltpu.make_async_copy(go_hbm.at[:, :, own_lanes], gv.at[0], load_sem.at[1]),
        pltpu.make_async_copy(pre_hbm.at[:, :, oth_lanes], pv.at[1], load_sem.at[2]),
        pltpu.make_async_copy(go_hbm.at[:, :, oth_lanes], gv.at[1], load_sem.at[3]),
        pltpu.make_async_copy(x_hbm, xv, load_sem.at[4]),
        pltpu.make_async_copy(sort_hbm.at[c], sv, load_sem.at[5]),
    ]
    for load in loads:
        load.start()

    sends = []

    def send(src, dst, send_sem, recv_sem, peer):
        copy = pltpu.make_async_remote_copy(
            src_ref=src, dst_ref=dst, send_sem=send_sem, recv_sem=recv_sem,
            device_id=peer, device_id_type=MESH,
        )
        copy.start()
        sends.append(copy)
        return copy

    rows_i = lax.broadcasted_iota(jnp.int32, (256, 256), 0)
    cols_i = lax.broadcasted_iota(jnp.int32, (256, 256), 1)
    flip = jnp.where(rows_i + cols_i == 255, 1.0, 0.0).astype(BF16)

    w_own = w_ref[:, :, own_lanes].astype(F32)
    w_oth = w_ref[:, :, oth_lanes].astype(F32)
    w0_own = w_own[:, 0, :]
    for i, row in enumerate((w_own[:, 1, :], w_oth[:, 1, :], w_oth[:, 0, :])):
        mirror_out[i] = jnp.concatenate([row, jnp.zeros((16 - K, 256), F32)], axis=0).astype(BF16)

    zeros = jnp.zeros((2, HALO, 512), F32)
    for padded in (gp, gfp):
        padded[:, 0:HALO, :] = zeros
        padded[:, HALO + 256 : 2 * HALO + 256, :] = zeros
    for half in range(2):
        loads[2 * half].wait()
        loads[2 * half + 1].wait()
        for seq in range(2):

            def slope(i, carry, half=half, seq=seq):
                rows = pl.ds(pl.multiple_of(i * 32, 32), 32)
                values = pv[half, seq, rows, :].astype(F32)
                grad = gv[half, seq, rows, :].astype(F32) * gelu_slope(values)
                place = pl.ds(pl.multiple_of(HALO + i * 32, 8), 32)
                gp[seq, place, half * 256 : half * 256 + 256] = grad.astype(BF16).astype(F32)
                return carry

            lax.fori_loop(0, 8, slope, 0)
    edge_out[0] = gp[:, 256 : 256 + HALO, :].reshape(2 * HALO, 512).astype(BF16)
    edge_out[1] = gp[:, HALO : 2 * HALO, :].reshape(2 * HALO, 512).astype(BF16)

    for seq in range(2):
        main = gp[seq, HALO : HALO + 256, :].astype(BF16)
        gfp[seq, HALO : HALO + 256, 0:256] = dot(main[:, 256:512], flip, 1, 0)
        gfp[seq, HALO : HALO + 256, 256:512] = dot(main[:, 0:256], flip, 1, 0)
    loads[4].wait()
    loads[5].wait()
    for seq in range(2):
        sorted_x = dot(sv[...], xv[seq], 1, 1).astype(BF16)
        xt[:, seq * 256 : seq * 256 + 256] = sorted_x[0:256]
        xt[:, 512 + seq * 256 : 768 + seq * 256] = sorted_x[256:512]
    for k in range(K):
        for seq in range(2):
            rk[k, seq * 256 : seq * 256 + 256, :] = gp[seq, 12 - k : 268 - k, :].astype(BF16)
            rk[k, 512 + seq * 256 : 768 + seq * 256, :] = gfp[seq, 4 + k : 260 + k, :].astype(BF16)

    for end, start in enumerate((0, 248)):
        ends = [xv[seq, start : start + 8, :].astype(F32) for seq in range(2)]
        x_out[end] = jnp.concatenate(ends, axis=0).astype(BF16)

    pl.semaphore_wait(barrier, len(peers))
    mirror = [
        send(mirror_out.at[i], mirror_in.at[i], m_s.at[i], m_r.at[i], peer)
        for i, peer in enumerate((mirror_a, mirror_b, twin))
    ]
    edges = [
        pltpu.make_async_remote_copy(
            src_ref=edge_out.at[i // 2], dst_ref=edge_in.at[i],
            send_sem=h_s.at[i], recv_sem=h_r.at[i],
            device_id=peer, device_id_type=MESH,
        )
        for i, peer in enumerate(beside)
    ]
    last_pos, first_pos = pos == 7, pos == 0
    for side, at_end in enumerate((last_pos, first_pos)):

        @pl.when(jnp.logical_not(at_end))
        def _(side=side):
            edges[2 * side].start()
            edges[2 * side + 1].start()

    x_ends = send(x_out, x_in, x_s.at[0], x_r.at[0], twin)

    def inner(k, carry):
        terms = dot(xt[...], rk[k], 1, 0)
        sf[k] = terms[:, 0:256].reshape(4, 4, 16, 256)
        for a in range(4):
            for b in range(4):
                rows = slice((a * 4 + b) * 16, (a * 4 + b) * 16 + 16)
                sd[k, b, a] = terms[rows, 256:512].astype(BF16)
        return carry

    twin_copies = []
    for group in range(GROUPS):
        lax.fori_loop(group * TAPS, group * TAPS + TAPS, inner, 0, unroll=True)
        taps = pl.ds(group * TAPS, TAPS)
        twin_copies.append(send(sd.at[taps], dr.at[taps], rd_s.at[group], rd_r.at[group], twin))

    for copy in mirror:
        copy.wait_recv()
    rev_a = dot(mirror_in[0], flip, 1, 0)
    rev_b = dot(mirror_in[1], flip, 1, 0)
    w0_oth = mirror_in[2].astype(F32)
    for k in range(K):
        zb[k, pl.ds(2 * z + c, 1), :] = w0_own[k : k + 1] + rev_a[8 - k : 9 - k]
        zb[k, pl.ds(2 * z + 1 - c, 1), :] = w0_oth[k : k + 1] + rev_b[8 - k : 9 - k]
    mine = pl.ds(2 * z, 2)
    z_gather = [
        send(zb.at[:, mine, :], zb.at[:, mine, :], z_s.at[i], z_r.at[i], peer)
        for i, peer in enumerate(z_peers)
    ]

    x_ends.wait_recv()
    blank = jnp.zeros((32, 512), BF16)
    for i in range(2):
        even_rows = jnp.concatenate([x_out[1 - i], x_in[1 - i], blank], axis=0)
        odd_rows = jnp.concatenate([blank, x_out[i], x_in[i]], axis=0)
        xe[i] = (dot(sv[0:256, :], even_rows, 1, 1) + dot(sv[256:512, :], odd_rows, 1, 1)).astype(BF16)
    for side, at_end in enumerate((first_pos, last_pos)):

        @pl.when(jnp.logical_not(at_end))
        def _(side=side):
            edges[2 * side].wait_recv()
            edges[2 * side + 1].wait_recv()

    border = [
        [jnp.where(at_end, 0.0, edge_in[2 * side + core].astype(F32)) for core in range(2)]
        for side, at_end in enumerate((first_pos, last_pos))
    ]
    low, high = [
        [
            border[side][core][seq * HALO : seq * HALO + HALO, core * 256 : core * 256 + 256]
            for core in range(2)
            for seq in range(2)
        ]
        for side in range(2)
    ]
    reverse_of = jnp.concatenate(
        [
            border[side][core][:, 256 - core * 256 : 512 - core * 256]
            for side in range(2)
            for core in range(2)
        ],
        axis=0,
    ).astype(BF16)
    reverse_of = dot(reverse_of, flip, 1, 0)
    blank = jnp.zeros((HALO, 256), F32)
    for seq in range(4):
        rev_low = reverse_of[seq * HALO : seq * HALO + HALO]
        rev_high = reverse_of[(4 + seq) * HALO : (5 + seq) * HALO]
        for i, parts in enumerate(
            ((blank, high[seq]), (rev_low, blank), (low[seq], blank), (blank, rev_high))
        ):
            edge_pad[i, seq, 0:HALO, :] = parts[0]
            edge_pad[i, seq, HALO : 2 * HALO, :] = parts[1]
    for k in range(K):
        first, second = (0, 1) if k <= 4 else (2, 3)
        start_1, start_2 = (4 - k, 4 + k) if k <= 4 else (12 - k, k - 4)
        rows_1 = [edge_pad[first, seq, start_1 : start_1 + 8, :] for seq in range(4)]
        rows_2 = [edge_pad[second, seq, start_2 : start_2 + 8, :] for seq in range(4)]
        edge_rows[k] = jnp.concatenate(rows_1 + rows_2, axis=0).astype(BF16)

    def chip_sum(group):
        twin_copies[group].wait_recv()

        def one(k, carry):
            terms = dot(xe[k // 5], edge_rows[k], 1, 0).reshape(4, 4, 16, 256)
            total = sf[k] + dr[k].astype(F32) + terms
            sf[k] = total
            qs[k] = total.astype(BF16)
            return carry

        lax.fori_loop(group * TAPS, group * TAPS + TAPS, one, 0)
        taps = pl.ds(group * TAPS, TAPS)
        return [
            send(
                qs.at[taps, (q + i) % 4], qr.at[i - 1, taps],
                rq_s.at[group, i - 1], rq_r.at[group, i - 1], q_peers[i - 1],
            )
            for i in range(1, 4)
        ]

    def q_sum(group, copies):
        for copy in copies:
            copy.wait_recv()

        def one(k, carry):
            total = sf[k, q] + qr[0, k].astype(F32) + qr[1, k].astype(F32) + qr[2, k].astype(F32)
            t1[k] = total
            ps[k] = total.astype(BF16)
            return carry

        lax.fori_loop(group * TAPS, group * TAPS + TAPS, one, 0)
        taps = pl.ds(group * TAPS, TAPS)
        return [
            send(
                ps.at[taps, (p + i) % 4], pr.at[i - 1, taps],
                rp_s.at[group, i - 1], rp_r.at[group, i - 1], p_peers[i - 1],
            )
            for i in range(1, 4)
        ]

    q_copies = [chip_sum(group) for group in range(GROUPS)]

    low = jnp.where(first_pos, 0.0, edge_in[0].astype(F32)).reshape(2, HALO, 512)
    high = jnp.where(last_pos, 0.0, edge_in[2].astype(F32)).reshape(2, HALO, 512)
    gp[:, 0:HALO, :] = low
    gp[:, HALO + 256 : 2 * HALO + 256, :] = high
    both = jnp.concatenate([low[0], low[1], high[0], high[1]], axis=0).astype(BF16)
    both = jnp.concatenate(
        [dot(both[:, 256:512], flip, 1, 0), dot(both[:, 0:256], flip, 1, 0)], axis=1
    )
    for seq in range(2):
        gfp[seq, 0:HALO, :] = both[seq * HALO : seq * HALO + HALO]
        gfp[seq, HALO + 256 : 2 * HALO + 256, :] = both[(2 + seq) * HALO : (3 + seq) * HALO]
    for k in range(K):
        for seq in range(2):
            for start in (0, 240):
                rk[k, seq * 256 + start : seq * 256 + start + 16, :] = gp[
                    seq, 12 - k + start : 28 - k + start, :
                ].astype(BF16)
                rk[k, 512 + seq * 256 + start : 528 + seq * 256 + start, :] = gfp[
                    seq, 4 + k + start : 20 + k + start, :
                ].astype(BF16)

    for copy in z_gather:
        copy.wait_recv()
    wb_own[:, q, p] = zb[...].astype(BF16)
    p_gather = [
        send(wb_own.at[:, q, p], wb_own.at[:, q, p], p_s.at[i], p_r.at[i], peer)
        for i, peer in enumerate(p_peers)
    ]
    p_copies = [q_sum(group, q_copies[group]) for group in range(GROUPS)]
    for copy in p_gather:
        copy.wait_recv()
    q_gather = [
        send(wb_own.at[:, q], wb_own.at[:, q], q_s.at[i], q_r.at[i], peer)
        for i, peer in enumerate(q_peers)
    ]
    d_gather = [send(wb_own.at[:, q], wb_oth.at[:, q], d_s.at[0], d_r.at[0], twin)]
    def p_sum(k, carry):
        zs[k] = t1[k, p] + pr[0, k].astype(F32) + pr[1, k].astype(F32) + pr[2, k].astype(F32)
        return carry

    z_scatter = []
    for group in range(GROUPS):
        for copy in p_copies[group]:
            copy.wait_recv()
        lax.fori_loop(group * TAPS, group * TAPS + TAPS, p_sum, 0)
        taps = pl.ds(group * TAPS, TAPS)
        for i, step in enumerate(z_steps):
            rows = pl.ds(2 * ((z + step) % 8), 2)
            z_scatter.append(
                send(
                    zs.at[taps, rows, :], zr.at[i, taps, rows, :],
                    rz_s.at[group, i], rz_r.at[group, i], z_peers[i],
                )
            )

    for i in range(1, 4):
        q_gather[i - 1].wait_recv()
        from_q = (q + 4 - i) % 4
        d_gather.append(
            send(wb_own.at[:, from_q], wb_oth.at[:, from_q], d_s.at[i], d_r.at[i], twin)
        )

    for copy in z_scatter:
        copy.wait_recv()
    for row, place in enumerate((2 * z + c, 2 * z + 1 - c)):
        total = zs[:, pl.ds(place, 1), :]
        for i in range(7):
            total = total + zr[i, :, pl.ds(place, 1), :]
        fs[row, 8:16, :] = jnp.zeros((8, 256), F32)
        for k in range(K):
            fs[row, k : k + 1, :] = total[k]
    final = [
        send(fs.at[1], fr.at[0], f_s.at[0], f_r.at[0], twin),
        send(fs.at[0], fr.at[1], f_s.at[1], f_r.at[1], mirror_a),
        send(fs.at[1], fr.at[2], f_s.at[2], f_r.at[2], mirror_b),
    ]

    total = jnp.zeros((1024, 256), F32)
    for k in range(K):
        total = total + dot(rk[k, :, 0:256], wb_own[k].reshape(256, 256), 1, 1)
    acc[...] = total

    for copy in d_gather:
        copy.wait_recv()

    def other_weight(k):
        return jnp.concatenate([wb_oth[k, b, a] for a in range(4) for b in range(4)], axis=0)

    total = acc[...]
    for k in range(K):
        total = total + dot(rk[k, :, 256:512], other_weight(k), 1, 1)
    acc[...] = total
    stores = []
    for seq in range(2):
        eo[:, 0:256] = acc[seq * 256 : seq * 256 + 256, :].astype(BF16)
        eo[:, 256:512] = acc[512 + seq * 256 : 768 + seq * 256, :].astype(BF16)
        gi[seq] = dot(eo[...], sv[...], 1, 0).astype(BF16)
        store = pltpu.make_async_copy(gi.at[seq], gi_hbm.at[seq], store_sem.at[seq])
        store.start()
        stores.append(store)

    for copy in final:
        copy.wait_recv()
    ow[0, :, 0, :] = fs[0, 0:K, :]
    ow[1, :, 0, :] = fr[0, 0:K, :]
    for half in range(2):
        value = fr[1 + half]
        high = value.astype(BF16)
        rest = value - high.astype(F32)
        mid = rest.astype(BF16)
        low = (rest - mid.astype(F32)).astype(BF16)
        reverse = dot(high, flip, 1, 0) + dot(mid, flip, 1, 0) + dot(low, flip, 1, 0)
        for k in range(K):
            ow[half, k, 1:2, :] = reverse[8 - k : 9 - k]
    for half, lanes in enumerate((own_lanes, oth_lanes)):
        store = pltpu.make_async_copy(ow.at[half], gw_hbm.at[:, :, lanes], store_sem.at[2 + half])
        store.start()
        stores.append(store)
    for copy in sends:
        copy.wait_send()
    for side, at_end in enumerate((last_pos, first_pos)):

        @pl.when(jnp.logical_not(at_end))
        def _(side=side):
            edges[2 * side].wait_send()
            edges[2 * side + 1].wait_send()

    for store in stores:
        store.wait()


def store_kernel(gi_in, gw_in, gi_out, gw_out):
    gi_out[...] = gi_in[...]
    gw_out[...] = gw_in[...]


def on_device(inputs, pre_act, grad_out, weight):
    sorts = jnp.asarray(channel_orders())
    dma = pltpu.SemaphoreType.DMA
    vmem = pltpu.VMEM
    grad_input, grad_weight = pl.pallas_call(
        kernel,
        out_shape=(
            jax.ShapeDtypeStruct((2, 256, 512), BF16),
            jax.ShapeDtypeStruct((K, 2, 512), F32),
        ),
        in_specs=[pl.BlockSpec(memory_space=vmem)] + [pl.BlockSpec(memory_space=pl.ANY)] * 4,
        out_specs=[pl.BlockSpec(memory_space=pl.ANY)] * 2,
        scratch_shapes=[
            vmem((2, 2, 256, 256), BF16),
            vmem((2, 2, 256, 256), BF16),
            vmem((2, 256, 512), BF16),
            vmem((512, 512), BF16),
            vmem((2, 256 + 2 * HALO, 512), F32),
            vmem((2, 256 + 2 * HALO, 512), F32),
            vmem((256, 1024), BF16),
            vmem((2, 256, 64), BF16),
            vmem((2, 16, 512), BF16),
            vmem((2, 16, 512), BF16),
            vmem((K, 1024, 512), BF16),
            vmem((2, 2 * HALO, 512), BF16),
            vmem((4, 2 * HALO, 512), BF16),
            vmem((4, 4, 2 * HALO, 256), F32),
            vmem((K, 64, 256), BF16),
            vmem((3, 16, 256), BF16),
            vmem((3, 16, 256), BF16),
            vmem((K, 16, 256), F32),
            vmem((K, 4, 4, 16, 256), BF16),
            vmem((K, 4, 4, 16, 256), BF16),
            vmem((K, 4, 4, 16, 256), F32),
            vmem((K, 4, 4, 16, 256), BF16),
            vmem((K, 4, 4, 16, 256), BF16),
            vmem((K, 4, 4, 16, 256), BF16),
            vmem((3, K, 4, 16, 256), BF16),
            vmem((K, 4, 16, 256), F32),
            vmem((K, 4, 16, 256), BF16),
            vmem((3, K, 16, 256), BF16),
            vmem((K, 16, 256), F32),
            vmem((7, K, 16, 256), F32),
            vmem((2, 16, 256), F32),
            vmem((3, 16, 256), F32),
            vmem((2, K, 2, 256), F32),
            vmem((1024, 256), F32),
            vmem((256, 512), BF16),
            vmem((2, 256, 512), BF16),
            dma((6,)), dma((4,)),
            dma((3,)), dma((3,)), dma((4,)), dma((4,)), dma((1,)), dma((1,)), dma((7,)), dma((7,)),
            dma((3,)), dma((3,)), dma((3,)), dma((3,)), dma((4,)), dma((4,)),
            dma((GROUPS,)), dma((GROUPS,)), dma((GROUPS, 3)), dma((GROUPS, 3)),
            dma((GROUPS, 3)), dma((GROUPS, 3)), dma((GROUPS, 7)), dma((GROUPS, 7)), dma((3,)), dma((3,)),
        ],
        compiler_params=pltpu.CompilerParams(
            collective_id=0, has_side_effects=True, vmem_limit_bytes=56 << 20
        ),
        name="conv_backward",
    )(jnp.transpose(weight, (1, 0, 2)), pre_act, grad_out, inputs, sorts)
    grad_input, grad_weight = pl.pallas_call(
        store_kernel,
        out_shape=(
            jax.ShapeDtypeStruct((2, 256, 512), BF16),
            jax.ShapeDtypeStruct((K, 2, 512), F32),
        ),
        in_specs=[pl.BlockSpec(memory_space=vmem)] * 2,
        out_specs=[pl.BlockSpec(memory_space=vmem)] * 2,
        name="store",
    )(grad_input, grad_weight)
    return grad_input, jnp.transpose(grad_weight, (1, 0, 2))


def solution(mesh):
    placed = (
        P("dp", "pos", None),
        P("dp", "pos", None),
        P("dp", "pos", None),
        P(("dp", "pos"), None, None),
    )
    return jax.shard_map(
        on_device,
        mesh=mesh,
        in_specs=placed,
        out_specs=(P("dp", "pos", None), P(("dp", "pos"), None, None)),
        check_vma=False,
    )
```

time: 56.2 us -> 53 us (0.943)
  local copies, waits for them, and re-layouts: 4.7 us -> 0 us
  Pallas kernels: 50.5 us -> 52.2 us
    unnamed x2 -> x0, local copies, waits for them, and re-layouts: 3.21 us -> none
    pallas_call x0 -> x1, Pallas kernels: none -> 1.87 us  [on_device(): pl.pallas_call(store_kernel, out_shape=(jax.ShapeDtypeStruct((2, 256, 512...]
    pallas_call x1 -> x0, local copies, waits for them, and re-layouts: 1.49 us -> none  [on_device(): pl.pallas_call(kernel, out_shape=(jax.ShapeDtypeStruct((2, 256, 512), BF1...]
where the time goes in v2:
time: 53 us; the launch traced here: 52.8 us
  Pallas kernels  52.2 us (98%)
  between operations  0.64 us (1%)
    pallas_call x1, Pallas kernels, on_device(): pl.pallas_call(kernel, out_shape=(jax.ShapeDtypeStruct((2, 256, 512), BF1...  50.3 us
    pallas_call x1, Pallas kernels, on_device(): pl.pallas_call(store_kernel, out_shape=(jax.ShapeDtypeStruct((2, 256, 512...  1.87 us

profile of v2, /device:TPU:32, one launch (start us, length us, event | category | flops | bytes accessed | tf_op | source)
XLA Modules:
  0.0 52.8 jit_solution(10964439648001841897)
XLA Ops:
  0.6 50.3 %conv_backward.1 = (bf16[2,256,512]{2,1,0:T(8,128)(2,1)}, f32[9,2,512]{2,1,0:T(2,128)}) custom-call(bf16[9,2,512]{2,1,0:T(2,128)(2,1)} %bitcast.2, bf16[2,256,512]{2,1,0:T(8,128)(2,1)} %pre_hbm.1, bf16[2,256,512]{2,1,0:T(8,128)(2,1)} %go_hbm.1, bf16[2,256,512]{2,1,0:T(8,128)(2,1)} %x_hbm.1, bf16[2,512,512]{2,1,0:T(8,128)(2,1)} %constant.2.clone.sort_hbm), custom_call_target="tpu_custom_call" | custom-call | tf_op jit(solution)/shard_map/conv_backward/pallas_call | solution.py:434
  50.9 1.9 %store.1 = (bf16[2,256,512]{2,1,0:T(8,128)(2,1)}, f32[9,2,512]{2,1,0:T(2,128)}) custom-call(bf16[2,256,512]{2,1,0:T(8,128)(2,1)} %get-tuple-element.6.gi_in, f32[9,2,512]{2,1,0:T(2,128)} %get-tuple-element.7.gw_in), custom_call_target="tpu_custom_call" | custom-call | tf_op jit(solution)/shard_map/store/pallas_call | solution.py:490

commit v3 on v2

--- a/solution.py
+++ b/solution.py
@@ -45,11 +45,11 @@
 
 
 def kernel(
-    w_ref, pre_hbm, go_hbm, x_hbm, sort_hbm, gi_hbm, gw_hbm,
-    pv, gv, xv, sv, gp, gfp, xt, xe, x_out, x_in, rk, edge_out, edge_in, edge_pad, edge_rows,
+    w_hbm, pre_hbm, go_hbm, x_hbm, sort_hbm, gi, gw,
+    w_ref, pv, gv, xv, sv, gp, gfp, xt, xe, x_out, x_in, rk, edge_out, edge_in, edge_pad, edge_rows,
     mirror_out, mirror_in, zb, wb_own, wb_oth,
-    sf, sd, dr, qs, qr, t1, ps, pr, zs, zr, fs, fr, ow, acc, eo, gi,
-    load_sem, store_sem, m_s, m_r, h_s, h_r, x_s, x_r, z_s, z_r, p_s, p_r, q_s, q_r, d_s, d_r,
+    sf, sd, dr, qs, qr, t1, ps, pr, zs, zr, fs, fr, acc, eo,
+    load_sem, m_s, m_r, h_s, h_r, x_s, x_r, z_s, z_r, p_s, p_r, q_s, q_r, d_s, d_r,
     rd_s, rd_r, rq_s, rq_r, rp_s, rp_r, rz_s, rz_r, f_s, f_r,
 ):
     dp, pos = lax.axis_index("dp"), lax.axis_index("pos")
@@ -82,11 +82,17 @@
         pltpu.make_async_copy(go_hbm.at[:, :, oth_lanes], gv.at[1], load_sem.at[3]),
         pltpu.make_async_copy(x_hbm, xv, load_sem.at[4]),
         pltpu.make_async_copy(sort_hbm.at[c], sv, load_sem.at[5]),
+        pltpu.make_async_copy(w_hbm, w_ref, load_sem.at[6]),
     ]
     for load in loads:
         load.start()
 
     sends = []
+
+    def drain():
+        while sends:
+            sends.pop(0).wait_send()
+
 
     def send(src, dst, send_sem, recv_sem, peer):
         copy = pltpu.make_async_remote_copy(
@@ -101,12 +107,6 @@
     cols_i = lax.broadcasted_iota(jnp.int32, (256, 256), 1)
     flip = jnp.where(rows_i + cols_i == 255, 1.0, 0.0).astype(BF16)
 
-    w_own = w_ref[:, :, own_lanes].astype(F32)
-    w_oth = w_ref[:, :, oth_lanes].astype(F32)
-    w0_own = w_own[:, 0, :]
-    for i, row in enumerate((w_own[:, 1, :], w_oth[:, 1, :], w_oth[:, 0, :])):
-        mirror_out[i] = jnp.concatenate([row, jnp.zeros((16 - K, 256), F32)], axis=0).astype(BF16)
-
     zeros = jnp.zeros((2, HALO, 512), F32)
     for padded in (gp, gfp):
         padded[:, 0:HALO, :] = zeros
@@ -125,24 +125,17 @@
                 return carry
 
             lax.fori_loop(0, 8, slope, 0)
+    loads[6].wait()
+    w_own = w_ref[:, :, own_lanes].astype(F32)
+    w_oth = w_ref[:, :, oth_lanes].astype(F32)
+    w0_own = w_own[:, 0, :]
+    for i, row in enumerate((w_own[:, 1, :], w_oth[:, 1, :], w_oth[:, 0, :])):
+        mirror_out[i] = jnp.concatenate([row, jnp.zeros((16 - K, 256), F32)], axis=0).astype(BF16)
+
     edge_out[0] = gp[:, 256 : 256 + HALO, :].reshape(2 * HALO, 512).astype(BF16)
     edge_out[1] = gp[:, HALO : 2 * HALO, :].reshape(2 * HALO, 512).astype(BF16)
 
-    for seq in range(2):
-        main = gp[seq, HALO : HALO + 256, :].astype(BF16)
-        gfp[seq, HALO : HALO + 256, 0:256] = dot(main[:, 256:512], flip, 1, 0)
-        gfp[seq, HALO : HALO + 256, 256:512] = dot(main[:, 0:256], flip, 1, 0)
     loads[4].wait()
-    loads[5].wait()
-    for seq in range(2):
-        sorted_x = dot(sv[...], xv[seq], 1, 1).astype(BF16)
-        xt[:, seq * 256 : seq * 256 + 256] = sorted_x[0:256]
-        xt[:, 512 + seq * 256 : 768 + seq * 256] = sorted_x[256:512]
-    for k in range(K):
-        for seq in range(2):
-            rk[k, seq * 256 : seq * 256 + 256, :] = gp[seq, 12 - k : 268 - k, :].astype(BF16)
-            rk[k, 512 + seq * 256 : 768 + seq * 256, :] = gfp[seq, 4 + k : 260 + k, :].astype(BF16)
-
     for end, start in enumerate((0, 248)):
         ends = [xv[seq, start : start + 8, :].astype(F32) for seq in range(2)]
         x_out[end] = jnp.concatenate(ends, axis=0).astype(BF16)
@@ -169,6 +162,20 @@
             edges[2 * side + 1].start()
 
     x_ends = send(x_out, x_in, x_s.at[0], x_r.at[0], twin)
+
+    for seq in range(2):
+        main = gp[seq, HALO : HALO + 256, :].astype(BF16)
+        gfp[seq, HALO : HALO + 256, 0:256] = dot(main[:, 256:512], flip, 1, 0)
+        gfp[seq, HALO : HALO + 256, 256:512] = dot(main[:, 0:256], flip, 1, 0)
+    loads[5].wait()
+    for seq in range(2):
+        sorted_x = dot(sv[...], xv[seq], 1, 1).astype(BF16)
+        xt[:, seq * 256 : seq * 256 + 256] = sorted_x[0:256]
+        xt[:, 512 + seq * 256 : 768 + seq * 256] = sorted_x[256:512]
+    for k in range(K):
+        for seq in range(2):
+            rk[k, seq * 256 : seq * 256 + 256, :] = gp[seq, 12 - k : 268 - k, :].astype(BF16)
+            rk[k, 512 + seq * 256 : 768 + seq * 256, :] = gfp[seq, 4 + k : 260 + k, :].astype(BF16)
 
     def inner(k, carry):
         terms = dot(xt[...], rk[k], 1, 0)
@@ -185,6 +192,12 @@
         taps = pl.ds(group * TAPS, TAPS)
         twin_copies.append(send(sd.at[taps], dr.at[taps], rd_s.at[group], rd_r.at[group], twin))
 
+    x_ends.wait_recv()
+    blank = jnp.zeros((32, 512), BF16)
+    for i in range(2):
+        even_rows = jnp.concatenate([x_out[1 - i], x_in[1 - i], blank], axis=0)
+        odd_rows = jnp.concatenate([blank, x_out[i], x_in[i]], axis=0)
+        xe[i] = (dot(sv[0:256, :], even_rows, 1, 1) + dot(sv[256:512, :], odd_rows, 1, 1)).astype(BF16)
     for copy in mirror:
         copy.wait_recv()
     rev_a = dot(mirror_in[0], flip, 1, 0)
@@ -199,12 +212,6 @@
         for i, peer in enumerate(z_peers)
     ]
 
-    x_ends.wait_recv()
-    blank = jnp.zeros((32, 512), BF16)
-    for i in range(2):
-        even_rows = jnp.concatenate([x_out[1 - i], x_in[1 - i], blank], axis=0)
-        odd_rows = jnp.concatenate([blank, x_out[i], x_in[i]], axis=0)
-        xe[i] = (dot(sv[0:256, :], even_rows, 1, 1) + dot(sv[256:512, :], odd_rows, 1, 1)).astype(BF16)
     for side, at_end in enumerate((first_pos, last_pos)):
 
         @pl.when(jnp.logical_not(at_end))
@@ -353,15 +360,17 @@
             send(wb_own.at[:, from_q], wb_oth.at[:, from_q], d_s.at[i], d_r.at[i], twin)
         )
 
-    for copy in z_scatter:
-        copy.wait_recv()
-    for row, place in enumerate((2 * z + c, 2 * z + 1 - c)):
-        total = zs[:, pl.ds(place, 1), :]
-        for i in range(7):
-            total = total + zr[i, :, pl.ds(place, 1), :]
-        fs[row, 8:16, :] = jnp.zeros((8, 256), F32)
-        for k in range(K):
-            fs[row, k : k + 1, :] = total[k]
+    fs[:, 8:16, :] = jnp.zeros((2, 8, 256), F32)
+    for group in range(GROUPS):
+        for copy in z_scatter[group * 7 : group * 7 + 7]:
+            copy.wait_recv()
+        taps = slice(group * TAPS, group * TAPS + TAPS)
+        for row, place in enumerate((2 * z + c, 2 * z + 1 - c)):
+            total = zs[taps, pl.ds(place, 1), :]
+            for i in range(7):
+                total = total + zr[i, taps, pl.ds(place, 1), :]
+            for k in range(TAPS):
+                fs[row, group * TAPS + k : group * TAPS + k + 1, :] = total[k]
     final = [
         send(fs.at[1], fr.at[0], f_s.at[0], f_r.at[0], twin),
         send(fs.at[0], fr.at[1], f_s.at[1], f_r.at[1], mirror_a),
@@ -383,48 +392,32 @@
     for k in range(K):
         total = total + dot(rk[k, :, 256:512], other_weight(k), 1, 1)
     acc[...] = total
-    stores = []
     for seq in range(2):
         eo[:, 0:256] = acc[seq * 256 : seq * 256 + 256, :].astype(BF16)
         eo[:, 256:512] = acc[512 + seq * 256 : 768 + seq * 256, :].astype(BF16)
         gi[seq] = dot(eo[...], sv[...], 1, 0).astype(BF16)
-        store = pltpu.make_async_copy(gi.at[seq], gi_hbm.at[seq], store_sem.at[seq])
-        store.start()
-        stores.append(store)
-
+
+    drain()
     for copy in final:
         copy.wait_recv()
-    ow[0, :, 0, :] = fs[0, 0:K, :]
-    ow[1, :, 0, :] = fr[0, 0:K, :]
-    for half in range(2):
-        value = fr[1 + half]
-        high = value.astype(BF16)
-        rest = value - high.astype(F32)
-        mid = rest.astype(BF16)
-        low = (rest - mid.astype(F32)).astype(BF16)
-        reverse = dot(high, flip, 1, 0) + dot(mid, flip, 1, 0) + dot(low, flip, 1, 0)
+    gw[:, 0, own_lanes] = fs[0, 0:K, :]
+    gw[:, 0, oth_lanes] = fr[0, 0:K, :]
+    value = fr[1:3].reshape(32, 256)
+    high = value.astype(BF16)
+    rest = value - high.astype(F32)
+    mid = rest.astype(BF16)
+    low = (rest - mid.astype(F32)).astype(BF16)
+    reverse = dot(jnp.concatenate([high, mid, low], axis=0), flip, 1, 0)
+    reverse = reverse[0:32] + reverse[32:64] + reverse[64:96]
+    for half, lanes in enumerate((own_lanes, oth_lanes)):
         for k in range(K):
-            ow[half, k, 1:2, :] = reverse[8 - k : 9 - k]
-    for half, lanes in enumerate((own_lanes, oth_lanes)):
-        store = pltpu.make_async_copy(ow.at[half], gw_hbm.at[:, :, lanes], store_sem.at[2 + half])
-        store.start()
-        stores.append(store)
-    for copy in sends:
-        copy.wait_send()
+            gw[k, 1:2, lanes] = reverse[half * 16 + 8 - k : half * 16 + 9 - k]
     for side, at_end in enumerate((last_pos, first_pos)):
 
         @pl.when(jnp.logical_not(at_end))
         def _(side=side):
             edges[2 * side].wait_send()
             edges[2 * side + 1].wait_send()
-
-    for store in stores:
-        store.wait()
-
-
-def store_kernel(gi_in, gw_in, gi_out, gw_out):
-    gi_out[...] = gi_in[...]
-    gw_out[...] = gw_in[...]
 
 
 def on_device(inputs, pre_act, grad_out, weight):
@@ -433,13 +426,11 @@
     vmem = pltpu.VMEM
     grad_input, grad_weight = pl.pallas_call(
         kernel,
-        out_shape=(
-            jax.ShapeDtypeStruct((2, 256, 512), BF16),
-            jax.ShapeDtypeStruct((K, 2, 512), F32),
-        ),
-        in_specs=[pl.BlockSpec(memory_space=vmem)] + [pl.BlockSpec(memory_space=pl.ANY)] * 4,
-        out_specs=[pl.BlockSpec(memory_space=pl.ANY)] * 2,
+        out_shape=(vmem((2, 256, 512), BF16), vmem((K, 2, 512), F32)),
+        in_specs=[pl.BlockSpec(memory_space=pl.ANY)] * 5,
+        out_specs=[pl.BlockSpec(memory_space=vmem)] * 2,
         scratch_shapes=[
+            vmem((K, 2, 512), BF16),
             vmem((2, 2, 256, 256), BF16),
             vmem((2, 2, 256, 256), BF16),
             vmem((2, 256, 512), BF16),
@@ -472,11 +463,9 @@
             vmem((7, K, 16, 256), F32),
             vmem((2, 16, 256), F32),
             vmem((3, 16, 256), F32),
-            vmem((2, K, 2, 256), F32),
             vmem((1024, 256), F32),
             vmem((256, 512), BF16),
-            vmem((2, 256, 512), BF16),
-            dma((6,)), dma((4,)),
+            dma((7,)),
             dma((3,)), dma((3,)), dma((4,)), dma((4,)), dma((1,)), dma((1,)), dma((7,)), dma((7,)),
             dma((3,)), dma((3,)), dma((3,)), dma((3,)), dma((4,)), dma((4,)),
             dma((GROUPS,)), dma((GROUPS,)), dma((GROUPS, 3)), dma((GROUPS, 3)),
@@ -487,16 +476,6 @@
         ),
         name="conv_backward",
     )(jnp.transpose(weight, (1, 0, 2)), pre_act, grad_out, inputs, sorts)
-    grad_input, grad_weight = pl.pallas_call(
-        store_kernel,
-        out_shape=(
-            jax.ShapeDtypeStruct((2, 256, 512), BF16),
-            jax.ShapeDtypeStruct((K, 2, 512), F32),
-        ),
-        in_specs=[pl.BlockSpec(memory_space=vmem)] * 2,
-        out_specs=[pl.BlockSpec(memory_space=vmem)] * 2,
-        name="store",
-    )(grad_input, grad_weight)
     return grad_input, jnp.transpose(grad_weight, (1, 0, 2))
 
 

time: 53 us -> 50.8 us (0.958)
  Pallas kernels: 52.2 us -> 48.7 us
  local copies, waits for them, and re-layouts: 0 us -> 1.41 us
    pallas_call x2 -> x1, Pallas kernels: 52.2 us -> 48.7 us  [on_device(): pl.pallas_call(kernel, out_shape=(vmem((2, 256, 512), BF16), vmem((K, 2,...]
    unnamed x0 -> x2, local copies, waits for them, and re-layouts: none -> 1.41 us
where the time goes in v3:
time: 50.8 us; the launch traced here: 50.7 us
  Pallas kernels  48.7 us (96%)
  local copies, waits for them, and re-layouts  1.41 us (3%)
  between operations  0.64 us (1%)
    pallas_call x1, Pallas kernels, on_device(): pl.pallas_call(kernel, out_shape=(vmem((2, 256, 512), BF16), vmem((K, 2,...  48.7 us
    unnamed x2, local copies, waits for them, and re-layouts  1.41 us

profile of v3, /device:TPU:32, one launch (start us, length us, event | category | flops | bytes accessed | tf_op | source)
XLA Modules:
  0.0 50.7 jit_solution(16071889039565012188)
XLA Ops:
  0.6 48.7 %conv_backward.1 = (bf16[2,256,512]{2,1,0:T(8,128)(2,1)S(1)}, f32[9,2,512]{2,1,0:T(2,128)S(1)}) custom-call(bf16[9,2,512]{2,1,0:T(2,128)(2,1)} %bitcast.3, bf16[2,256,512]{2,1,0:T(8,128)(2,1)} %pre_hbm.1, bf16[2,256,512]{2,1,0:T(8,128)(2,1)} %go_hbm.1, bf16[2,256,512]{2,1,0:T(8,128)(2,1)} %x_hbm.1, bf16[2,512,512]{2,1,0:T(8,128)(2,1)} %constant.2.clone.sort_hbm), custom_call_target="tpu_custom_call" | custom-call | tf_op jit(solution)/shard_map/conv_backward/pallas_call | solution.py:427
  49.3 0.8 %copy.9 = bf16[2,256,512]{2,1,0:T(8,128)(2,1)} copy(bf16[2,256,512]{2,1,0:T(8,128)(2,1)S(1)} %get-tuple-element.6) | data formatting | bytes 1048576
  50.1 0.6 %copy.10 = f32[2,9,512]{2,0,1:T(2,128)} copy(f32[2,9,512]{2,0,1:T(2,128)S(1)} %bitcast.2) | data formatting | bytes 73728

commit v4 on v3

--- a/solution.py
+++ b/solution.py
@@ -266,14 +266,14 @@
             qs[k] = total.astype(BF16)
             return carry
 
-        lax.fori_loop(group * TAPS, group * TAPS + TAPS, one, 0)
+        lax.fori_loop(group * TAPS, group * TAPS + TAPS, one, 0, unroll=True)
         taps = pl.ds(group * TAPS, TAPS)
         return [
             send(
                 qs.at[taps, (q + i) % 4], qr.at[i - 1, taps],
                 rq_s.at[group, i - 1], rq_r.at[group, i - 1], q_peers[i - 1],
             )
-            for i in range(1, 4)
+            for i in (2, 1, 3)
         ]
 
     def q_sum(group, copies):
@@ -286,14 +286,14 @@
             ps[k] = total.astype(BF16)
             return carry
 
-        lax.fori_loop(group * TAPS, group * TAPS + TAPS, one, 0)
+        lax.fori_loop(group * TAPS, group * TAPS + TAPS, one, 0, unroll=True)
         taps = pl.ds(group * TAPS, TAPS)
         return [
             send(
                 ps.at[taps, (p + i) % 4], pr.at[i - 1, taps],
                 rp_s.at[group, i - 1], rp_r.at[group, i - 1], p_peers[i - 1],
             )
-            for i in range(1, 4)
+            for i in (2, 1, 3)
         ]
 
     q_copies = [chip_sum(group) for group in range(GROUPS)]
@@ -342,7 +342,7 @@
     for group in range(GROUPS):
         for copy in p_copies[group]:
             copy.wait_recv()
-        lax.fori_loop(group * TAPS, group * TAPS + TAPS, p_sum, 0)
+        lax.fori_loop(group * TAPS, group * TAPS + TAPS, p_sum, 0, unroll=True)
         taps = pl.ds(group * TAPS, TAPS)
         for i, step in enumerate(z_steps):
             rows = pl.ds(2 * ((z + step) % 8), 2)

time: 50.8 us -> 49.3 us (0.970)
  Pallas kernels: 48.7 us -> 47.2 us
    pallas_call x1, Pallas kernels: 48.7 us -> 47.2 us  [on_device(): pl.pallas_call(kernel, out_shape=(vmem((2, 256, 512), BF16), vmem((K, 2,...]
where the time goes in v4:
time: 49.3 us; the launch traced here: 49.2 us
  Pallas kernels  47.2 us (96%)
  local copies, waits for them, and re-layouts  1.41 us (3%)
  between operations  0.64 us (1%)
    pallas_call x1, Pallas kernels, on_device(): pl.pallas_call(kernel, out_shape=(vmem((2, 256, 512), BF16), vmem((K, 2,...  47.2 us
    unnamed x2, local copies, waits for them, and re-layouts  1.41 us

profile of v4, /device:TPU:32, one launch (start us, length us, event | category | flops | bytes accessed | tf_op | source)
XLA Modules:
  0.0 49.2 jit_solution(11007999688981064226)
XLA Ops:
  0.6 47.2 %conv_backward.1 = (bf16[2,256,512]{2,1,0:T(8,128)(2,1)S(1)}, f32[9,2,512]{2,1,0:T(2,128)S(1)}) custom-call(bf16[9,2,512]{2,1,0:T(2,128)(2,1)} %bitcast.3, bf16[2,256,512]{2,1,0:T(8,128)(2,1)} %pre_hbm.1, bf16[2,256,512]{2,1,0:T(8,128)(2,1)} %go_hbm.1, bf16[2,256,512]{2,1,0:T(8,128)(2,1)} %x_hbm.1, bf16[2,512,512]{2,1,0:T(8,128)(2,1)} %constant.2.clone.sort_hbm), custom_call_target="tpu_custom_call" | custom-call | tf_op jit(solution)/shard_map/conv_backward/pallas_call | solution.py:427
  47.8 0.8 %copy.9 = bf16[2,256,512]{2,1,0:T(8,128)(2,1)} copy(bf16[2,256,512]{2,1,0:T(8,128)(2,1)S(1)} %get-tuple-element.6) | data formatting | bytes 1048576
  48.6 0.6 %copy.10 = f32[2,9,512]{2,0,1:T(2,128)} copy(f32[2,9,512]{2,0,1:T(2,128)S(1)} %bitcast.2) | data formatting | bytes 73728

commit v5 on v4

--- a/solution.py
+++ b/solution.py
@@ -60,8 +60,9 @@
     q = y * (1 - c) + x * c
     z_steps = (4, 3, 5, 2, 6, 1, 7)
     z_peers = [device(x, y, (z + i) % 8, c) for i in z_steps]
-    p_peers = [device((x + i * (1 - c)) % 4, (y + i * c) % 4, z, c) for i in range(1, 4)]
-    q_peers = [device((x + i * c) % 4, (y + i * (1 - c)) % 4, z, c) for i in range(1, 4)]
+    p_steps = (2, 1, 3)
+    p_peers = [device((x + i * (1 - c)) % 4, (y + i * c) % 4, z, c) for i in p_steps]
+    q_peers = [device((x + i * c) % 4, (y + i * (1 - c)) % 4, z, c) for i in p_steps]
     twin = device(x, y, z, 1 - c)
     mirror_a = device(3 - x, 3 - y, 7 - z, 1 - c)
     mirror_b = device(3 - x, 3 - y, 7 - z, c)
@@ -141,10 +142,6 @@
         x_out[end] = jnp.concatenate(ends, axis=0).astype(BF16)
 
     pl.semaphore_wait(barrier, len(peers))
-    mirror = [
-        send(mirror_out.at[i], mirror_in.at[i], m_s.at[i], m_r.at[i], peer)
-        for i, peer in enumerate((mirror_a, mirror_b, twin))
-    ]
     edges = [
         pltpu.make_async_remote_copy(
             src_ref=edge_out.at[i // 2], dst_ref=edge_in.at[i],
@@ -161,6 +158,10 @@
             edges[2 * side].start()
             edges[2 * side + 1].start()
 
+    mirror = [
+        send(mirror_out.at[i], mirror_in.at[i], m_s.at[i], m_r.at[i], peer)
+        for i, peer in enumerate((mirror_a, mirror_b, twin))
+    ]
     x_ends = send(x_out, x_in, x_s.at[0], x_r.at[0], twin)
 
     for seq in range(2):
@@ -270,10 +271,10 @@
         taps = pl.ds(group * TAPS, TAPS)
         return [
             send(
-                qs.at[taps, (q + i) % 4], qr.at[i - 1, taps],
-                rq_s.at[group, i - 1], rq_r.at[group, i - 1], q_peers[i - 1],
+                qs.at[taps, (q + step) % 4], qr.at[i, taps],
+                rq_s.at[group, i], rq_r.at[group, i], q_peers[i],
             )
-            for i in (2, 1, 3)
+            for i, step in enumerate(p_steps)
         ]
 
     def q_sum(group, copies):
@@ -290,10 +291,10 @@
         taps = pl.ds(group * TAPS, TAPS)
         return [
             send(
-                ps.at[taps, (p + i) % 4], pr.at[i - 1, taps],
-                rp_s.at[group, i - 1], rp_r.at[group, i - 1], p_peers[i - 1],
+                ps.at[taps, (p + step) % 4], pr.at[i, taps],
+                rp_s.at[group, i], rp_r.at[group, i], p_peers[i],
             )
-            for i in (2, 1, 3)
+            for i, step in enumerate(p_steps)
         ]
 
     q_copies = [chip_sum(group) for group in range(GROUPS)]
@@ -326,13 +327,14 @@
         send(wb_own.at[:, q, p], wb_own.at[:, q, p], p_s.at[i], p_r.at[i], peer)
         for i, peer in enumerate(p_peers)
     ]
-    p_copies = [q_sum(group, q_copies[group]) for group in range(GROUPS)]
+    p_copies = [q_sum(group, q_copies[group]) for group in range(GROUPS - 1)]
     for copy in p_gather:
         copy.wait_recv()
     q_gather = [
         send(wb_own.at[:, q], wb_own.at[:, q], q_s.at[i], q_r.at[i], peer)
         for i, peer in enumerate(q_peers)
     ]
+    p_copies.append(q_sum(GROUPS - 1, q_copies[GROUPS - 1]))
     d_gather = [send(wb_own.at[:, q], wb_oth.at[:, q], d_s.at[0], d_r.at[0], twin)]
     def p_sum(k, carry):
         zs[k] = t1[k, p] + pr[0, k].astype(F32) + pr[1, k].astype(F32) + pr[2, k].astype(F32)
@@ -353,11 +355,11 @@
                 )
             )
 
-    for i in range(1, 4):
-        q_gather[i - 1].wait_recv()
-        from_q = (q + 4 - i) % 4
+    for i in (1, 2, 0):
+        q_gather[i].wait_recv()
+        from_q = (q + 4 - p_steps[i]) % 4
         d_gather.append(
-            send(wb_own.at[:, from_q], wb_oth.at[:, from_q], d_s.at[i], d_r.at[i], twin)
+            send(wb_own.at[:, from_q], wb_oth.at[:, from_q], d_s.at[1 + i], d_r.at[1 + i], twin)
         )
 
     fs[:, 8:16, :] = jnp.zeros((2, 8, 256), F32)
@@ -372,9 +374,9 @@
             for k in range(TAPS):
                 fs[row, group * TAPS + k : group * TAPS + k + 1, :] = total[k]
     final = [
-        send(fs.at[1], fr.at[0], f_s.at[0], f_r.at[0], twin),
         send(fs.at[0], fr.at[1], f_s.at[1], f_r.at[1], mirror_a),
         send(fs.at[1], fr.at[2], f_s.at[2], f_r.at[2], mirror_b),
+        send(fs.at[1], fr.at[0], f_s.at[0], f_r.at[0], twin),
     ]
 
     total = jnp.zeros((1024, 256), F32)

time: 49.3 us -> 49.1 us (level)
  no operation moved by 1% of the time
where the time goes in v5:
time: 49.1 us; the launch traced here: 48.8 us
  Pallas kernels  46.8 us (95%)
  local copies, waits for them, and re-layouts  1.41 us (3%)
  between operations  0.64 us (1%)
    pallas_call x1, Pallas kernels, on_device(): pl.pallas_call(kernel, out_shape=(vmem((2, 256, 512), BF16), vmem((K, 2,...  46.8 us
    unnamed x2, local copies, waits for them, and re-layouts  1.41 us

profile of v5, /device:TPU:32, one launch (start us, length us, event | category | flops | bytes accessed | tf_op | source)
XLA Modules:
  0.0 48.8 jit_solution(6874126314620016050)
XLA Ops:
  0.6 46.8 %conv_backward.1 = (bf16[2,256,512]{2,1,0:T(8,128)(2,1)S(1)}, f32[9,2,512]{2,1,0:T(2,128)S(1)}) custom-call(bf16[9,2,512]{2,1,0:T(2,128)(2,1)} %bitcast.3, bf16[2,256,512]{2,1,0:T(8,128)(2,1)} %pre_hbm.1, bf16[2,256,512]{2,1,0:T(8,128)(2,1)} %go_hbm.1, bf16[2,256,512]{2,1,0:T(8,128)(2,1)} %x_hbm.1, bf16[2,512,512]{2,1,0:T(8,128)(2,1)} %constant.2.clone.sort_hbm), custom_call_target="tpu_custom_call" | custom-call | tf_op jit(solution)/shard_map/conv_backward/pallas_call | solution.py:429
  47.4 0.8 %copy.9 = bf16[2,256,512]{2,1,0:T(8,128)(2,1)} copy(bf16[2,256,512]{2,1,0:T(8,128)(2,1)S(1)} %get-tuple-element.6) | data formatting | bytes 1048576
  48.2 0.6 %copy.10 = f32[2,9,512]{2,0,1:T(2,128)} copy(f32[2,9,512]{2,0,1:T(2,128)S(1)} %bitcast.2) | data formatting | bytes 73728

commit v6 on v5

--- a/solution.py
+++ b/solution.py
@@ -299,6 +299,13 @@
 
     q_copies = [chip_sum(group) for group in range(GROUPS)]
 
+    for copy in z_gather:
+        copy.wait_recv()
+    wb_own[:, q, p] = zb[...].astype(BF16)
+    p_gather = [
+        send(wb_own.at[:, q, p], wb_own.at[:, q, p], p_s.at[i], p_r.at[i], peer)
+        for i, peer in enumerate(p_peers)
+    ]
     low = jnp.where(first_pos, 0.0, edge_in[0].astype(F32)).reshape(2, HALO, 512)
     high = jnp.where(last_pos, 0.0, edge_in[2].astype(F32)).reshape(2, HALO, 512)
     gp[:, 0:HALO, :] = low
@@ -320,13 +327,6 @@
                     seq, 4 + k + start : 20 + k + start, :
                 ].astype(BF16)
 
-    for copy in z_gather:
-        copy.wait_recv()
-    wb_own[:, q, p] = zb[...].astype(BF16)
-    p_gather = [
-        send(wb_own.at[:, q, p], wb_own.at[:, q, p], p_s.at[i], p_r.at[i], peer)
-        for i, peer in enumerate(p_peers)
-    ]
     p_copies = [q_sum(group, q_copies[group]) for group in range(GROUPS - 1)]
     for copy in p_gather:
         copy.wait_recv()

time: 49.1 us -> 49.1 us (level)
  no operation moved by 1% of the time
where the time goes in v6:
time: 49.1 us; the launch traced here: 48.8 us
  Pallas kernels  46.8 us (95%)
  local copies, waits for them, and re-layouts  1.41 us (3%)
  between operations  0.64 us (1%)
    pallas_call x1, Pallas kernels, on_device(): pl.pallas_call(kernel, out_shape=(vmem((2, 256, 512), BF16), vmem((K, 2,...  46.8 us
    unnamed x2, local copies, waits for them, and re-layouts  1.41 us

profile of v6, /device:TPU:32, one launch (start us, length us, event | category | flops | bytes accessed | tf_op | source)
XLA Modules:
  0.0 48.8 jit_solution(13516033770835648584)
XLA Ops:
  0.6 46.8 %conv_backward.1 = (bf16[2,256,512]{2,1,0:T(8,128)(2,1)S(1)}, f32[9,2,512]{2,1,0:T(2,128)S(1)}) custom-call(bf16[9,2,512]{2,1,0:T(2,128)(2,1)} %bitcast.3, bf16[2,256,512]{2,1,0:T(8,128)(2,1)} %pre_hbm.1, bf16[2,256,512]{2,1,0:T(8,128)(2,1)} %go_hbm.1, bf16[2,256,512]{2,1,0:T(8,128)(2,1)} %x_hbm.1, bf16[2,512,512]{2,1,0:T(8,128)(2,1)} %constant.2.clone.sort_hbm), custom_call_target="tpu_custom_call" | custom-call | tf_op jit(solution)/shard_map/conv_backward/pallas_call | solution.py:429
  47.4 0.8 %copy.9 = bf16[2,256,512]{2,1,0:T(8,128)(2,1)} copy(bf16[2,256,512]{2,1,0:T(8,128)(2,1)S(1)} %get-tuple-element.6) | data formatting | bytes 1048576
  48.2 0.6 %copy.10 = f32[2,9,512]{2,0,1:T(2,128)} copy(f32[2,9,512]{2,0,1:T(2,128)S(1)} %bitcast.2) | data formatting | bytes 73728
